TPU v7x, 256 devices: a whole 4x4x8 slice. The times are simulated.
256 devices in a mesh: row: 8 (over z_lo, core), col: 32 (over y, z_hi, x).
Axes of the slice: x: 4, y: 4, z: 8 (z_hi: 2, z_lo: 4; z = z_hi * 4 + z_lo), core: 2. Of those that a mesh axis runs over, the one named last changes fastest.
Arguments:
- features: bfloat16 [32, 2048, 2048], P(None, 'col', 'row'), may hold values from -6 to 6
- cotangent: bfloat16 [32, 2048, 2048], P(None, 'col', 'row'), may hold values from -6 to 6
- mask: int32 [2048], replicated, may hold values 0 or 1
- w_conv: bfloat16 [3, 3, 32, 32], replicated, may hold values from -0.375 to 0.375
- w_point: bfloat16 [32, 32], replicated, may hold values from -1 to 1
- bias: float32 [32], replicated, may hold values from -3 to 3
Outputs:
- feature_grad: bfloat16 [32, 2048, 2048], P(None, 'col', 'row')
- conv_grad: float32 [3, 3, 32, 32], replicated
- point_grad: float32 [32, 32], replicated
- bias_grad: float32 [32], replicated
Inputs may be any that keep to these rules, and one draw needn't show every extreme that they name: `mask`: 1 marks a mappable bin, 0 an unmappable one.
All inputs are finite; a program needn't handle non-finite values.
Results may differ from a plain program's by a relative error of at most 0.008.
Values may be sent and summed in bfloat16 or wider, within the bound.
A program may use at most 64 MiB of HBM per device.

v0:
```python
import jax
import jax.numpy as jnp
from jax import lax
from jax.experimental import pallas as pl
from jax.experimental.pallas import tpu as pltpu
from jax.sharding import PartitionSpec as P

F32, BF16 = jnp.float32, jnp.bfloat16
MESH = pl.DeviceIdType.MESH
ROWS, COLS = 8, 32
TILE = 256
TAPS = 3 * TILE
TILES = 8
GROUP = 16
SLICES = ((0, 3), (3, 1))
NT = (((1,), (1,)), ((), ()))
TN = (((0,), (0,)), ((), ()))


def iota(shape, dim):
    return lax.broadcasted_iota(jnp.int32, shape, dim)


def dot(x, y):
    return jnp.dot(x, y, preferred_element_type=F32)


def dot_nt(x, y):
    return lax.dot_general(x, y, NT, preferred_element_type=F32)


def dot_tn(x, y):
    return lax.dot_general(x, y, TN, preferred_element_type=F32)


def one_hot(where):
    return where.astype(F32).astype(BF16)


def at(start, size):
    return pl.ds(pl.multiple_of(start, size), size)


def sigmoid(v):
    return 1.0 / (1.0 + jnp.exp(-v))


def pack(tile, bottom):
    v = tile.reshape(16, 2, 8, 256)
    low = iota((16, 8, 256), 1) < 4
    if bottom:
        v = jnp.where(low, v[:, 0], pltpu.roll(v[:, 1], 4, 1))
    else:
        v = jnp.where(low, pltpu.roll(v[:, 0], 4, 1), v[:, 1])
    return v.reshape(128, 256).astype(BF16)


def unpack(packed, bottom):
    width = packed.shape[1]
    v = packed.astype(F32).reshape(16, 8, width)
    turned = pltpu.roll(v, 4, 1)
    low = iota((16, 8, width), 1) < 4
    if bottom:
        pair = [jnp.where(low, v, 0.0), jnp.where(low, turned, 0.0)]
    else:
        pair = [jnp.where(low, 0.0, turned), jnp.where(low, 0.0, v)]
    return jnp.stack(pair, axis=1).reshape(TILE, width)


def kernel(
    feat_hbm, cot_hbm, mask_hbm, wconv_hbm, wpoint_hbm, bias_hbm,
    fg_hbm, sums_hbm,
    mask_ref, wconv_ref, wpoint_ref, bias_ref,
    feat, cot, mir_send, relay, mir_recv, act, grad, res, res_half, slope, pre_slope, post, gnat,
    mat_f, mat_b, mat_p, keep, prev, csum, psum, bsum, out,
    ns_send, ew_send, corner_send, ns_recv, ew_recv, corner_recv, payload, part1, sum1, part2, sum2, part3,
    in_sem, out_sem, spread_ssem, spread_rsem, mir_ssem, mir_rsem, halo_ssem, halo_rsem, red_ssem, red_rsem,
):
    r, c = lax.axis_index("row"), lax.axis_index("col")
    a, b = lax.div(c, 4), lax.rem(c, 4)
    y, zh = lax.div(c, 8), lax.rem(a, 2)
    group_a, group_b = zh * 8 + r, y * 4 + b

    def mirror_to(x, row):
        return {"row": 2 * row + zh, "col": 4 * r + x}

    def mirror_from(x, row):
        return {"row": a, "col": 8 * row + 4 * lax.rem(r, 2) + x}

    def member_a(m):
        return {"row": lax.rem(m, 8), "col": y * 8 + lax.div(m, 8) * 4 + b}

    def member_b(m):
        return {"row": r, "col": lax.div(m, 4) * 8 + zh * 4 + lax.rem(m, 4)}

    def beside(dr, dc):
        return {"row": lax.rem(r + dr + ROWS, ROWS), "col": lax.rem(c + dc + COLS, COLS)}

    own_mirror = a == r
    sides = [(0, 1), (0, -1), (1, 0), (-1, 0), (1, 1), (-1, 1), (1, -1), (-1, -1)]

    barrier = pltpu.get_barrier_semaphore()

    def greet(device):
        pl.semaphore_signal(barrier, inc=1, device_id=device, device_id_type=MESH)

    @pl.when(jnp.logical_not(own_mirror))
    def _():
        greet(mirror_to(b, y))
        greet(mirror_from(b, y))

    def greet_mirrors(n, _):
        x, row = lax.rem(b + lax.div(n, 4), 4), lax.rem(y + n, 4)
        greet(mirror_to(x, row))
        greet(mirror_from(x, row))
        return 0

    lax.fori_loop(1, GROUP, greet_mirrors, 0)
    for dr, dc in sides:
        greet(beside(dr, dc))

    def greet_groups(d, _):
        greet(member_a(lax.rem(group_a + d, GROUP)))
        greet(member_b(lax.rem(group_b + d, GROUP)))
        return 0

    lax.fori_loop(1, GROUP, greet_groups, 0)

    load_cot = pltpu.make_async_copy(cot_hbm, cot, in_sem.at[0])
    load_feat = pltpu.make_async_copy(feat_hbm, feat, in_sem.at[1])
    loads = [
        pltpu.make_async_copy(source, target, in_sem.at[2 + n])
        for n, (source, target) in enumerate(
            [(mask_hbm, mask_ref), (wconv_hbm, wconv_ref), (wpoint_hbm, wpoint_ref), (bias_hbm, bias_ref)]
        )
    ]
    load_cot.start()
    load_feat.start()
    for copy in loads:
        copy.start()

    load_cot.wait()
    ident = (iota((256, 256), 0) == iota((256, 256), 1)).astype(BF16)

    def turn(g, _):
        block = cot[at(4 * g, 4)].reshape(256, 256)
        turned = dot_nt(ident, block).astype(BF16)
        mir_send[:, :, at(16 * g, 16), :] = turned.reshape(4, 4, 16, 256)
        return 0

    lax.fori_loop(0, 8, turn, 0)

    low = iota((32, 8, 256), 1) < 4

    centre = {0: lambda t: TAPS * t + TILE, 1: lambda t: TILE * t}

    def put(phase, t, tile):
        ref = (act, grad)[phase]
        ref[at(centre[phase](t), TILE), :] = tile.reshape(TILE, 256).astype(BF16)

    def activations():
        load_feat.wait()
        prev[...] = jnp.zeros_like(prev)

        def activate(k, _):
            x = feat[:, at(16 * k, 16), :].astype(F32)
            for h in range(2):
                t = 2 * k + h
                v = x[:, 8 * h : 8 * h + 8, :]
                s = sigmoid(v)
                slope[at(TILE * t, TILE), :] = (s * (1.0 + v * (1.0 - s))).reshape(TILE, 256)
                turned = pltpu.roll(v * s, 4, 1)
                put(0, t, jnp.where(low, prev[...], turned))
                prev[...] = turned
            return 0

        lax.fori_loop(0, 4, activate, 0)
        put(0, TILES, jnp.where(low, prev[...], 0.0))

    def halo_copies(phase):
        diagonal = corner_send.at[phase]
        pairs = [
            (ns_send.at[phase, 1], ns_recv.at[phase, 0]),
            (ns_send.at[phase, 0], ns_recv.at[phase, 1]),
            (ew_send.at[phase, 48:96], ew_recv.at[phase, 48:96]),
            (ew_send.at[phase, 0:48], ew_recv.at[phase, 0:48]),
            (diagonal, corner_recv.at[phase, 0]),
            (diagonal, corner_recv.at[phase, 1]),
            (diagonal, corner_recv.at[phase, 2]),
            (diagonal, corner_recv.at[phase, 3]),
        ]
        return [
            pltpu.make_async_remote_copy(
                src_ref=src,
                dst_ref=dst,
                send_sem=halo_ssem.at[phase, n],
                recv_sem=halo_rsem.at[phase, n],
                device_id=beside(*sides[n]),
                device_id_type=MESH,
            )
            for n, (src, dst) in enumerate(pairs)
        ]

    def halo_pack(phase):
        ref = (act, grad)[phase]
        first, last = centre[phase](0), centre[phase](TILES)
        ns_send[phase, 0] = pack(ref[first : first + TILE, :].astype(F32), False)
        ns_send[phase, 1] = pack(ref[last : last + TILE, :].astype(F32), True)
        row, col = iota((96, 256), 0), iota((96, 256), 1)

        def gather(t, total):
            pick = ((row == 4 * t + col) & (col < 4)) | ((row == 4 * t + col - 204) & (col >= 252))
            return total + dot_nt(one_hot(pick), ref[at(centre[phase](t), TILE), :])

        edge = lax.fori_loop(0, TILES + 1, gather, jnp.zeros((96, 256), F32))
        ew_send[phase] = edge.astype(BF16)
        row, col = iota((8, 256), 0), iota((8, 256), 1)
        pick = one_hot(((row == col) & (row < 4)) | ((row == col - 248) & (row >= 4)))
        corners = [dot_nt(pick, ns_send[phase, n]) for n in range(2)]
        corner_send[phase] = jnp.concatenate(corners, axis=0).astype(BF16)

    up, down, left, right = c > 0, c < COLS - 1, r > 0, r < ROWS - 1

    def only(flag, value):
        return jnp.where(flag, value, 0.0)

    def halo_edge(phase):
        row, lane = iota((96, 128), 0), iota((96, 128), 1)
        straight = ((row == lane) & (row < 48) & right) | ((row == lane - 16) & (lane >= 64) & left)
        edge = dot_tn(ew_recv[phase], one_hot(straight))
        row, lane = iota((16, 128), 0), iota((16, 128), 1)

        def place(n, first, start, flag):
            hit = (row >= first) & (row < first + 4) & (lane == row - first + start) & flag
            return dot_tn(corner_recv[phase, n], one_hot(hit))

        above = place(0, 12, 64, left & up) + place(1, 8, 0, right & up)
        below = place(2, 4, 96, left & down) + place(3, 0, 32, right & down)
        return (edge + unpack(above, True) + unpack(below, False)).astype(BF16)

    def halo_rows(phase):
        above = only(up, unpack(ns_recv[phase, 0], True))
        below = only(down, unpack(ns_recv[phase, 1], False))
        return above, below

    def act_fill():
        above, below = halo_rows(0)
        for t, value in ((0, above), (TILES, below)):
            rows = slice(TAPS * t + TILE, TAPS * t + 2 * TILE)
            act[rows, :] = (act[rows, :].astype(F32) + value).astype(BF16)
        edge = halo_edge(0)
        from_j, to_j = iota((256, 512), 0), iota((256, 512), 1)
        shift = one_hot(((to_j < 256) & (from_j == to_j - 4)) | ((to_j >= 256) & (from_j == to_j - 252)))
        lane, col = iota((128, 512), 0), iota((128, 512), 1)

        def spread(t, _):
            place = ((col < 4) & (lane == 64 + 4 * t + col)) | ((col >= 508) & (lane == 4 * t + col - 508))
            both = dot(act[at(TAPS * t + TILE, TILE), :], shift) + dot(edge, one_hot(place))
            act[at(TAPS * t, TILE), :] = both[:, :256].astype(BF16)
            act[at(TAPS * t + 2 * TILE, TILE), :] = both[:, 256:].astype(BF16)
            return 0

        lax.fori_loop(0, TILES + 1, spread, 0)

    def rows_of(part):
        return pl.ds(*SLICES[part])

    def spread_copy(part, n):
        dx, dy = lax.div(n, 4), lax.rem(n, 4)
        to_x, to_y = lax.rem(b + dx, 4), lax.rem(y + dy, 4)
        return pltpu.make_async_remote_copy(
            src_ref=mir_send.at[to_x, rows_of(part), at(32 * to_y, 32), :],
            dst_ref=relay.at[y, to_x, rows_of(part)],
            send_sem=spread_ssem.at[part, n],
            recv_sem=spread_rsem.at[part, n],
            device_id=member_b(4 * to_y + b),
            device_id_type=MESH,
        )

    def relay_copy(part, n):
        dx, dy = lax.div(n, 4), lax.rem(n, 4)
        to_x, from_y = lax.rem(b + dx, 4), lax.rem(y - dy + 4, 4)
        return pltpu.make_async_remote_copy(
            src_ref=relay.at[from_y, to_x, rows_of(part)],
            dst_ref=mir_recv.at[b, rows_of(part), at(32 * y, 32), :],
            send_sem=mir_ssem.at[part, n],
            recv_sem=mir_rsem.at[part, 4 * y + b],
            device_id=mirror_to(to_x, from_y),
            device_id_type=MESH,
        )

    def own_copy(part):
        return pltpu.make_async_copy(
            relay.at[y, b, rows_of(part)],
            mir_recv.at[b, rows_of(part), at(32 * y, 32), :],
            mir_rsem.at[part, 4 * y + b],
        )

    def arrival(part, n):
        from_y, from_x = lax.div(n, 4), lax.rem(n, 4)
        return pltpu.make_async_remote_copy(
            src_ref=relay.at[from_y, from_x, rows_of(part)],
            dst_ref=mir_recv.at[from_x, rows_of(part), at(32 * from_y, 32), :],
            send_sem=mir_ssem.at[part, n],
            recv_sem=mir_rsem.at[part, n],
            device_id=mirror_from(from_x, from_y),
            device_id_type=MESH,
        )

    for x in range(4):
        relay[y, x] = mir_send[x, :, at(32 * y, 32), :]
    pl.semaphore_wait(barrier, 2 * GROUP + 8 + 2 * (GROUP - 1) - 2 * own_mirror.astype(jnp.int32))

    def relayed(n):
        return lax.rem(n, 4) > 0

    def each(part, step, count=GROUP):
        lax.fori_loop(0, count, lambda n, _: step(part, n), 0)

    def send_spread(part, n):
        @pl.when(relayed(n))
        def _():
            spread_copy(part, n).start()

        return 0

    def start_own(part, m):
        stays = own_mirror & (m == 0)

        @pl.when(stays)
        def _():
            own_copy(part).start()

        @pl.when(jnp.logical_not(stays))
        def _():
            relay_copy(part, 4 * m).start()

        return 0

    def pass_on(part, n):
        @pl.when(relayed(n))
        def _():
            spread_copy(part, n).wait_recv()
            relay_copy(part, n).start()

        return 0

    def sent(part, n):
        @pl.when(relayed(n))
        def _():
            spread_copy(part, n).wait_send()

        @pl.when(jnp.logical_not(own_mirror & (n == 0)))
        def _():
            relay_copy(part, n).wait_send()

        return 0

    for part in range(len(SLICES)):
        each(part, send_spread)
    for part in range(len(SLICES)):
        each(part, start_own, 4)
    activations()
    halo_pack(0)
    for copy in halo_copies(0):
        copy.start()

    each(0, pass_on)

    for copy in loads:
        copy.wait()

    spread_out = (lax.div(iota((256, 32), 0), 8) == iota((256, 32), 1)).astype(F32).astype(BF16)
    spread_in = (lax.div(iota((32, 256), 1), 8) == iota((32, 256), 0)).astype(F32).astype(BF16)
    row_out, row_in = lax.rem(iota((256, 256), 0), 8), lax.rem(iota((256, 256), 1), 8)

    def expand(w, turned):
        rows = dot_nt(spread_out, w) if turned else dot(spread_out, w)
        return dot(rows.astype(BF16), spread_in)

    def banded(taps):
        near = jnp.where(row_in == row_out, taps[0], 0.0) + jnp.where(row_in == row_out + 4, taps[1], 0.0)
        far = jnp.where(row_in == row_out, taps[2], 0.0) + jnp.where(row_in == row_out - 4, taps[1], 0.0)
        return near.astype(BF16), far.astype(BF16)

    for tap in range(3):
        near, far = banded([expand(wconv_ref[n, tap], False) for n in range(3)])
        mat_f[:, tap * TILE : (tap + 1) * TILE] = near
        mat_f[:, TAPS + tap * TILE : TAPS + (tap + 1) * TILE] = far
        near, far = banded([expand(wconv_ref[2 - n, 2 - tap], True) for n in range(3)])
        mat_b[tap * TILE : (tap + 1) * TILE, :TILE] = near
        mat_b[tap * TILE : (tap + 1) * TILE, TILE:] = far
    mat_p[...] = jnp.where(row_in == row_out, expand(wpoint_ref[...], True), 0.0).astype(BF16)

    bias_col = jnp.sum(
        jnp.where(lax.div(iota((256, 32), 0), 8) == iota((256, 32), 1), bias_ref[...], 0.0), axis=1, keepdims=True
    )
    mask_row = mask_ref[:, at(256 * a, 256)].astype(F32)
    diagonal = iota((64, 256), 1) == iota((64, 256), 0) + 64 * b
    row_keep = jnp.sum(jnp.where(diagonal, mask_row, 0.0), axis=1, keepdims=True)
    keep[...] = row_keep * (0.5 * mask_ref[:, at(256 * r, 256)].astype(F32))

    csum[...] = jnp.zeros_like(csum)
    psum[...] = jnp.zeros_like(psum)
    bsum[...] = jnp.zeros_like(bsum)

    each(1, pass_on)
    for copy in halo_copies(0):
        copy.wait_recv()
    act_fill()

    def forward(t, _):
        v = dot(mat_f[...], act[pl.ds(pl.multiple_of(TAPS * t, TAPS), 2 * TAPS), :])
        v = v + bias_col
        s = sigmoid(v)
        post[at(TILE * t, TILE), :] = (v * s).astype(BF16)
        pre_slope[at(TILE * t, TILE), :] = s * (1.0 + v * (1.0 - s))
        return 0

    lax.fori_loop(0, TILES, forward, 0)

    prev[...] = jnp.zeros_like(prev)
    left_half = iota((8, 8, 128), 2) < 64

    def arrive(part, n):
        stays = own_mirror & (n == 4 * y + b)

        @pl.when(stays)
        def _():
            own_copy(part).wait()

        @pl.when(jnp.logical_not(stays))
        def _():
            arrival(part, n).wait_recv()

        return 0

    def chunk(k, _):
        for part, (first, _) in enumerate(SLICES):

            @pl.when(k == first)
            def _():
                each(part, arrive)

        here = cot[:, at(16 * k, 16), :].astype(F32)
        keep_rows = keep[at(16 * k, 16), :]
        got = [mir_recv[n, k].astype(F32).reshape(8, 16, 256) for n in range(4)]
        for h in range(2):
            t = 2 * k + h
            part = [v[:, 8 * h : 8 * h + 8, :] for v in got]
            quads = []
            for m in range(4):
                cols = slice(128 * (m // 2), 128 * (m // 2) + 128)
                pieces = []
                for n in (0, 2):
                    one, two = part[n][:, :, cols], part[n + 1][:, :, cols]
                    if m % 2 == 0:
                        pieces.append(jnp.where(left_half, one, pltpu.roll(two, 64, 2)))
                    else:
                        pieces.append(jnp.where(left_half, pltpu.roll(one, 64, 2), two))
                quads.append(jnp.concatenate(pieces, axis=2))
            mirrored = jnp.stack(quads, axis=1).reshape(32, 8, 256)
            residual = keep_rows[8 * h : 8 * h + 8][None] * (here[:, 8 * h : 8 * h + 8, :] + mirrored)
            residual = residual.reshape(TILE, 256)
            half = residual.astype(BF16)
            res[at(TILE * t, TILE), :] = residual
            res_half[at(TILE * t, TILE), :] = half
            g = pre_slope[at(TILE * t, TILE), :] * dot(mat_p[...], half)
            gnat[at(TILE * t, TILE), :] = g.astype(BF16)
            turned = pltpu.roll(g.reshape(32, 8, 256), 4, 1)
            put(1, t, jnp.where(low, prev[...], turned))
            prev[...] = turned

        @pl.when(k == 3)
        def _():
            put(1, TILES, jnp.where(low, prev[...], 0.0))

        total, point, line = csum[...], psum[...], bsum[...]
        for h in range(2):
            t = 2 * k + h
            g = gnat[at(TILE * t, TILE), :]
            total = total + dot_nt(g, act[pl.ds(pl.multiple_of(TAPS * t, TAPS), 2 * TAPS), :])
            point = point + dot_nt(res_half[at(TILE * t, TILE), :], post[at(TILE * t, TILE), :])
            wide = g.astype(F32)
            line = line + wide[:, :128] + wide[:, 128:]
        csum[...] = total
        psum[...] = point
        bsum[...] = line
        return 0

    lax.fori_loop(0, 4, chunk, 0)

    def exchange(stage, me, member, source, dst):
        def copy(d):
            to = lax.rem(me + d, GROUP)
            return pltpu.make_async_remote_copy(
                src_ref=source(to),
                dst_ref=dst.at[me],
                send_sem=red_ssem.at[stage, d],
                recv_sem=red_rsem.at[stage, d],
                device_id=member(to),
                device_id_type=MESH,
            )

        def start(d, _):
            copy(d).start()
            return 0

        def arrive(d, _):
            copy(d).wait_recv()
            return 0

        def leave(d, _):
            copy(d).wait_send()
            return 0

        if stage == 0:
            return (
                lambda m: copy(lax.rem(m - me + GROUP, GROUP)),
                lambda: lax.fori_loop(1, GROUP, arrive, 0),
                lambda: lax.fori_loop(1, GROUP, leave, 0),
            )
        return (
            lambda: lax.fori_loop(1, GROUP, start, 0),
            lambda: lax.fori_loop(1, GROUP, arrive, 0),
            lambda: lax.fori_loop(1, GROUP, leave, 0),
        )

    first_copy, arrive1, leave1 = exchange(0, group_a, member_a, lambda m: payload.at[m], part1)
    start2, arrive2, leave2 = exchange(1, group_b, member_b, lambda m: sum1, part2)
    start3, arrive3, leave3 = exchange(2, group_a, member_a, lambda m: sum2, part3)

    def send_payload(m):
        @pl.when(group_a == m)
        def _():
            part1[m] = payload[m]

        @pl.when(group_a != m)
        def _():
            first_copy(m).start()

    col_in = lax.div(iota((256, 128), 0), 8)
    col_out = iota((256, 128), 1)
    for quad in range(3):
        lanes = jnp.zeros((256, 128), F32)
        for slot in range(4):
            n = 4 * quad + slot
            if n > 9:
                continue
            if n == 9:
                v = jnp.where(row_in == row_out, psum[...], 0.0)
            else:
                row_tap, col_tap = n // 3, n % 3
                near = csum[:, col_tap * TILE : (col_tap + 1) * TILE]
                far = csum[:, TAPS + col_tap * TILE : TAPS + (col_tap + 1) * TILE]
                if row_tap == 0:
                    v = jnp.where(row_in == row_out, near, 0.0)
                elif row_tap == 2:
                    v = jnp.where(row_in == row_out, far, 0.0)
                else:
                    v = jnp.where(row_in == row_out + 4, near, 0.0) + jnp.where(row_in == row_out - 4, far, 0.0)
            pick = (col_out == 32 * slot + col_in).astype(F32).astype(BF16)
            high = v.astype(BF16)
            lanes = lanes + (dot(high, pick) + dot((v - high.astype(F32)).astype(BF16), pick))
        if quad == 2:
            line = jnp.sum(bsum[...], axis=1, keepdims=True)
            lanes = lanes + jnp.where((col_out >= 64) & (col_out < 96), line, 0.0)
        lanes = jnp.sum(lanes.reshape(32, 8, 128), axis=1)
        for o in range(4):
            payload[4 * quad + o] = lanes[8 * o : 8 * o + 8]
            send_payload(4 * quad + o)
    for o in range(12, GROUP):
        payload[o] = jnp.zeros((8, 128), F32)
        send_payload(o)

    def total_of(ref):
        total = ref[0]
        for n in range(1, GROUP):
            total = total + ref[n]
        return total

    halo_pack(1)
    for copy in halo_copies(1):
        copy.start()

    lane256 = iota((TILE, 256), 1)

    def over_taps(v):
        west = jnp.where(lane256 >= 4, pltpu.roll(v[:TILE], 4, 1), 0.0)
        east = jnp.where(lane256 < 252, pltpu.roll(v[2 * TILE :], 252, 1), 0.0)
        return v[TILE : 2 * TILE] + west + east

    def inner(t, _):
        v = dot(mat_b[...], grad[pl.ds(pl.multiple_of(TILE * t, TILE), 2 * TILE), :])
        pre_slope[at(TILE * t, TILE), :] = over_taps(v)
        return 0

    lax.fori_loop(0, 3, inner, 0)
    for part in range(len(SLICES)):
        each(part, sent)
    for copy in halo_copies(0):
        copy.wait_send()
    arrive1()
    sum1[...] = total_of(part1)
    part2[group_b] = sum1[...]
    start2()
    lax.fori_loop(3, TILES, inner, 0)
    leave1()
    arrive2()
    sum2[...] = total_of(part2)
    part3[group_a] = sum2[...]
    start3()

    leave2()
    for copy in halo_copies(1):
        copy.wait()
    above, below = halo_rows(1)
    pre_slope[:TILE, :] += over_taps(dot(mat_b[:, :TILE], above.astype(BF16)))
    pre_slope[TILE * (TILES - 1) :, :] += over_taps(dot(mat_b[:, TILE:], below.astype(BF16)))
    edge = halo_edge(1)
    from_west = dot(mat_b[:TILE, :TILE], edge) + pltpu.roll(dot(mat_b[:TILE, TILE:], edge), 124, 1)
    from_east = dot(mat_b[2 * TILE :, :TILE], edge) + pltpu.roll(dot(mat_b[2 * TILE :, TILE:], edge), 124, 1)
    lane128 = iota((TILE, 128), 1)
    outer = jnp.where(lane128 < 64, from_east, from_west)

    def store_out(k):
        rows = at(16 * k, 16)
        return pltpu.make_async_copy(out.at[:, rows, :], fg_hbm.at[:, rows, :], out_sem.at[k])

    def backward(k, _):
        halves = []
        for h in range(2):
            t = 2 * k + h
            west = jnp.where(lane128 < 4, pltpu.roll(outer, lax.rem(192 - 4 * t, 128), 1), 0.0)
            east = jnp.where(lane128 >= 124, pltpu.roll(outer, 124 - 4 * t, 1), 0.0)
            v = pre_slope[at(TILE * t, TILE), :] + jnp.concatenate([west, east], axis=1)
            v = res[at(TILE * t, TILE), :] + slope[at(TILE * t, TILE), :] * v
            halves.append(v.reshape(32, 8, 256))
        out[:, at(16 * k, 16), :] = jnp.concatenate(halves, axis=1).astype(BF16)
        store_out(k).start()
        return 0

    lax.fori_loop(0, 4, backward, 0)
    arrive3()

    store_sums = pltpu.make_async_copy(part3.at[0:12], sums_hbm, out_sem.at[4])
    store_sums.start()

    leave3()
    for k in range(4):
        store_out(k).wait()
    store_sums.wait()


def finish(
    fg_hbm, sums_hbm, out_hbm, conv_hbm, point_hbm, biasg_hbm, held, sums_ref, conv_ref, point_ref, biasg_ref, sem
):
    parts = [slice(8 * n, 8 * n + 8) for n in range(4)]
    loads = [pltpu.make_async_copy(fg_hbm.at[p], held.at[p], sem.at[0, n]) for n, p in enumerate(parts)]
    stores = [pltpu.make_async_copy(held.at[p], out_hbm.at[p], sem.at[1, n]) for n, p in enumerate(parts)]
    load_sums = pltpu.make_async_copy(sums_hbm, sums_ref, sem.at[2, 0])
    load_sums.start()
    for copy in loads:
        copy.start()
    for load, store in zip(loads, stores):
        load.wait()
        store.start()
    load_sums.wait()
    scale = 1.0 / 2048.0
    for quad in range(3):
        lanes = jnp.concatenate([sums_ref[4 * quad + o] for o in range(4)], axis=0) * scale
        for slot in range(4):
            n = 4 * quad + slot
            block = lanes if slot == 0 else pltpu.roll(lanes, 128 - 32 * slot, 1)
            if n < 9:
                conv_ref[n // 3, n % 3] = block[:, :32]
            elif n == 9:
                point_ref[...] = block[:, :32]
            elif n == 10:
                square = block[:, :32]
                biasg_ref[...] = jnp.sum(
                    jnp.where(iota((32, 32), 0) == iota((32, 32), 1), square, 0.0), axis=0, keepdims=True
                )
    small = [
        pltpu.make_async_copy(source, target, sem.at[2, 1 + n])
        for n, (source, target) in enumerate([(conv_ref, conv_hbm), (point_ref, point_hbm), (biasg_ref, biasg_hbm)])
    ]
    for copy in small:
        copy.start()
    for copy in stores + small:
        copy.wait()


def shards(features, cotangent, mask, w_conv, w_point, bias):
    hbm = pl.BlockSpec(memory_space=pl.ANY)
    big = (TILES * TILE, 256)
    fg, sums = pl.pallas_call(
        kernel,
        out_shape=(
            jax.ShapeDtypeStruct((32, 64, 256), BF16),
            jax.ShapeDtypeStruct((12, 8, 128), F32),
        ),
        in_specs=[hbm] * 6,
        out_specs=(hbm, hbm),
        scratch_shapes=[
            pltpu.VMEM((1, 2048), jnp.int32),
            pltpu.VMEM((3, 3, 32, 32), BF16),
            pltpu.VMEM((32, 32), BF16),
            pltpu.VMEM((1, 32), F32),
            pltpu.VMEM((32, 64, 256), BF16),
            pltpu.VMEM((32, 64, 256), BF16),
            pltpu.VMEM((4, 4, 128, 256), BF16),
            pltpu.VMEM((4, 4, 4, 32, 256), BF16),
            pltpu.VMEM((4, 4, 128, 256), BF16),
            pltpu.VMEM(((TILES + 1) * TAPS, 256), BF16),
            pltpu.VMEM(((TILES + 1) * TILE, 256), BF16),
            pltpu.VMEM(big, F32),
            pltpu.VMEM(big, BF16),
            pltpu.VMEM(big, F32),
            pltpu.VMEM(big, F32),
            pltpu.VMEM(big, BF16),
            pltpu.VMEM(big, BF16),
            pltpu.VMEM((TILE, 2 * TAPS), BF16),
            pltpu.VMEM((TAPS, 2 * TILE), BF16),
            pltpu.VMEM((TILE, TILE), BF16),
            pltpu.VMEM((64, 256), F32),
            pltpu.VMEM((32, 8, 256), F32),
            pltpu.VMEM((TILE, 2 * TAPS), F32),
            pltpu.VMEM((TILE, TILE), F32),
            pltpu.VMEM((TILE, 128), F32),
            pltpu.VMEM((32, 64, 256), BF16),
            pltpu.VMEM((2, 2, 128, 256), BF16),
            pltpu.VMEM((2, 96, 256), BF16),
            pltpu.VMEM((2, 16, 128), BF16),
            pltpu.VMEM((2, 2, 128, 256), BF16),
            pltpu.VMEM((2, 96, 256), BF16),
            pltpu.VMEM((2, 4, 16, 128), BF16),
            pltpu.VMEM((GROUP, 8, 128), F32),
            pltpu.VMEM((GROUP, 8, 128), F32),
            pltpu.VMEM((8, 128), F32),
            pltpu.VMEM((GROUP, 8, 128), F32),
            pltpu.VMEM((8, 128), F32),
            pltpu.VMEM((GROUP, 8, 128), F32),
            pltpu.SemaphoreType.DMA((6,)),
            pltpu.SemaphoreType.DMA((5,)),
            pltpu.SemaphoreType.DMA((len(SLICES), GROUP)),
            pltpu.SemaphoreType.DMA((len(SLICES), GROUP)),
            pltpu.SemaphoreType.DMA((len(SLICES), GROUP)),
            pltpu.SemaphoreType.DMA((len(SLICES), GROUP)),
            pltpu.SemaphoreType.DMA((2, 8)),
            pltpu.SemaphoreType.DMA((2, 8)),
            pltpu.SemaphoreType.DMA((3, GROUP)),
            pltpu.SemaphoreType.DMA((3, GROUP)),
        ],
        compiler_params=pltpu.CompilerParams(
            collective_id=0, has_side_effects=True, vmem_limit_bytes=56 * 1024 * 1024
        ),
        cost_estimate=pl.CostEstimate(flops=5_400_000_000, bytes_accessed=3 * 1024 * 1024, transcendentals=2_000_000),
    )(features, cotangent, mask.reshape(1, 2048), w_conv, w_point, bias.reshape(1, 32))
    fg, conv, point, bias_grad = pl.pallas_call(
        finish,
        out_shape=(
            jax.ShapeDtypeStruct((32, 64, 256), BF16),
            jax.ShapeDtypeStruct((3, 3, 32, 32), F32),
            jax.ShapeDtypeStruct((32, 32), F32),
            jax.ShapeDtypeStruct((1, 32), F32),
        ),
        in_specs=[hbm, hbm],
        out_specs=(hbm, hbm, hbm, hbm),
        scratch_shapes=[
            pltpu.VMEM((32, 64, 256), BF16),
            pltpu.VMEM((12, 8, 128), F32),
            pltpu.VMEM((3, 3, 32, 32), F32),
            pltpu.VMEM((32, 32), F32),
            pltpu.VMEM((1, 32), F32),
            pltpu.SemaphoreType.DMA((3, 4)),
        ],
    )(fg, sums)
    return fg, conv, point, bias_grad.reshape(32)


def solution(mesh):
    in_specs = (P(None, "col", "row"), P(None, "col", "row"), P(), P(), P(), P())
    out_specs = (P(None, "col", "row"), P(), P(), P())
    return jax.shard_map(shards, mesh=mesh, in_specs=in_specs, out_specs=out_specs, check_vma=False)
```

profile of v0, /device:TPU:1, one launch (start us, length us, event | category | flops | bytes accessed | tf_op | source)
XLA Modules:
  0.0 74.4 jit_solution(10838905165938099801)
XLA Ops:
  0.6 71.7 %shard_map.93 = (bf16[32,64,256]{2,1,0:T(8,128)(2,1)}, f32[12,8,128]{2,1,0:T(8,128)}) custom-call(bf16[32,64,256]{2,1,0:T(8,128)(2,1)} %feat_hbm.1, bf16[32,64,256]{2,1,0:T(8,128)(2,1)} %cot_hbm.1, s32[1,2048]{1,0:T(1,128)} %bitcast.3, bf16[3,3,32,32]{3,2,1,0:T(8,128)(2,1)} %wconv_hbm.1, bf16[32,32]{1,0:T(8,128)(2,1)} %wpoint_hbm.1, f32[1,32]{1,0:T(1,128)} %bitcast.4), custom_call_target="tpu_custom_call" | custom-call | flops 5400000000 | bytes 3145728 | tf_op jit(solution)/shard_map/pallas_call | solution.py:697
  72.3 2.1 %shard_map.94 = (bf16[32,64,256]{2,1,0:T(8,128)(2,1)}, f32[3,3,32,32]{3,2,1,0:T(8,128)}, f32[32,32]{1,0:T(8,128)}, f32[1,32]{1,0:T(1,128)}) custom-call(bf16[32,64,256]{2,1,0:T(8,128)(2,1)} %get-tuple-element.10.fg_hbm, f32[12,8,128]{2,1,0:T(8,128)} %get-tuple-element.11.sums_hbm), custom_call_target="tpu_custom_call" | custom-call | tf_op jit(solution)/shard_map/pallas_call | solution.py:760
where the time goes:
time: 74.5 us; the launch traced here: 74.4 us
  Pallas kernels  73.8 us (99%)
    pallas_call x1, Pallas kernels, shards(): pl.pallas_call(kernel, out_shape=(jax.ShapeDtypeStruct((32, 64, 256), BF1...  71.7 us
    pallas_call x1, Pallas kernels, shards(): pl.pallas_call(finish, out_shape=(jax.ShapeDtypeStruct((32, 64, 256), BF1...  2.09 us

commit v1 on v0

--- a/solution.py
+++ b/solution.py
@@ -12,6 +12,7 @@
 TAPS = 3 * TILE
 TILES = 8
 GROUP = 16
+FIRST, SECOND = 2, 5
 SLICES = ((0, 3), (3, 1))
 NT = (((1,), (1,)), ((), ()))
 TN = (((0,), (0,)), ((), ()))
@@ -491,51 +492,41 @@
     lax.fori_loop(0, 4, chunk, 0)
 
     def exchange(stage, me, member, source, dst):
-        def copy(d):
-            to = lax.rem(me + d, GROUP)
+        def copy(to):
             return pltpu.make_async_remote_copy(
                 src_ref=source(to),
                 dst_ref=dst.at[me],
-                send_sem=red_ssem.at[stage, d],
-                recv_sem=red_rsem.at[stage, d],
+                send_sem=red_ssem.at[stage],
+                recv_sem=red_rsem.at[stage],
                 device_id=member(to),
                 device_id_type=MESH,
             )
 
         def start(d, _):
-            copy(d).start()
+            copy(lax.rem(me + d, GROUP)).start()
             return 0
 
-        def arrive(d, _):
-            copy(d).wait_recv()
-            return 0
-
-        def leave(d, _):
-            copy(d).wait_send()
-            return 0
-
-        if stage == 0:
-            return (
-                lambda m: copy(lax.rem(m - me + GROUP, GROUP)),
-                lambda: lax.fori_loop(1, GROUP, arrive, 0),
-                lambda: lax.fori_loop(1, GROUP, leave, 0),
-            )
+        def wait(sem):
+            others = dst.at[0 : GROUP - 1]
+            pltpu.make_async_copy(others, others, sem.at[stage]).wait()
+
         return (
+            copy,
             lambda: lax.fori_loop(1, GROUP, start, 0),
-            lambda: lax.fori_loop(1, GROUP, arrive, 0),
-            lambda: lax.fori_loop(1, GROUP, leave, 0),
+            lambda: wait(red_rsem),
+            lambda: wait(red_ssem),
         )
 
-    first_copy, arrive1, leave1 = exchange(0, group_a, member_a, lambda m: payload.at[m], part1)
-    start2, arrive2, leave2 = exchange(1, group_b, member_b, lambda m: sum1, part2)
-    start3, arrive3, leave3 = exchange(2, group_a, member_a, lambda m: sum2, part3)
+    first_copy, _, arrive1, leave1 = exchange(0, group_b, member_b, lambda m: payload.at[m], part1)
+    _, start2, arrive2, leave2 = exchange(1, group_a, member_a, lambda m: sum1, part2)
+    _, start3, arrive3, leave3 = exchange(2, group_b, member_b, lambda m: sum2, part3)
 
     def send_payload(m):
-        @pl.when(group_a == m)
+        @pl.when(group_b == m)
         def _():
             part1[m] = payload[m]
 
-        @pl.when(group_a != m)
+        @pl.when(group_b != m)
         def _():
             first_copy(m).start()
 
@@ -595,23 +586,20 @@
         pre_slope[at(TILE * t, TILE), :] = over_taps(v)
         return 0
 
-    lax.fori_loop(0, 3, inner, 0)
-    for part in range(len(SLICES)):
-        each(part, sent)
-    for copy in halo_copies(0):
-        copy.wait_send()
+    lax.fori_loop(0, FIRST, inner, 0)
     arrive1()
     sum1[...] = total_of(part1)
-    part2[group_b] = sum1[...]
+    part2[group_a] = sum1[...]
     start2()
-    lax.fori_loop(3, TILES, inner, 0)
+    lax.fori_loop(FIRST, SECOND, inner, 0)
     leave1()
     arrive2()
     sum2[...] = total_of(part2)
-    part3[group_a] = sum2[...]
+    part3[group_b] = sum2[...]
     start3()
 
     leave2()
+    lax.fori_loop(SECOND, TILES, inner, 0)
     for copy in halo_copies(1):
         copy.wait()
     above, below = halo_rows(1)
@@ -641,6 +629,10 @@
         return 0
 
     lax.fori_loop(0, 4, backward, 0)
+    for part in range(len(SLICES)):
+        each(part, sent)
+    for copy in halo_copies(0):
+        copy.wait_send()
     arrive3()
 
     store_sums = pltpu.make_async_copy(part3.at[0:12], sums_hbm, out_sem.at[4])
@@ -749,8 +741,8 @@
             pltpu.SemaphoreType.DMA((len(SLICES), GROUP)),
             pltpu.SemaphoreType.DMA((2, 8)),
             pltpu.SemaphoreType.DMA((2, 8)),
-            pltpu.SemaphoreType.DMA((3, GROUP)),
-            pltpu.SemaphoreType.DMA((3, GROUP)),
+            pltpu.SemaphoreType.DMA((3,)),
+            pltpu.SemaphoreType.DMA((3,)),
         ],
         compiler_params=pltpu.CompilerParams(
             collective_id=0, has_side_effects=True, vmem_limit_bytes=56 * 1024 * 1024

time: 74.5 us -> 70.2 us (0.942)
  Pallas kernels: 73.8 us -> 69.5 us
    pallas_call x1, Pallas kernels: 71.7 us -> 67.4 us  [shards(): pl.pallas_call(kernel, out_shape=(jax.ShapeDtypeStruct((32, 64, 256), BF1...]
where the time goes in v1:
time: 70.2 us; the launch traced here: 70.1 us
  Pallas kernels  69.5 us (99%)
    pallas_call x1, Pallas kernels, shards(): pl.pallas_call(kernel, out_shape=(jax.ShapeDtypeStruct((32, 64, 256), BF1...  67.4 us
    pallas_call x1, Pallas kernels, shards(): pl.pallas_call(finish, out_shape=(jax.ShapeDtypeStruct((32, 64, 256), BF1...  2.09 us

profile of v1, /device:TPU:1, one launch (start us, length us, event | category | flops | bytes accessed | tf_op | source)
XLA Modules:
  0.0 70.1 jit_solution(11699376278917984316)
XLA Ops:
  0.6 67.4 %shard_map.93 = (bf16[32,64,256]{2,1,0:T(8,128)(2,1)}, f32[12,8,128]{2,1,0:T(8,128)}) custom-call(bf16[32,64,256]{2,1,0:T(8,128)(2,1)} %feat_hbm.1, bf16[32,64,256]{2,1,0:T(8,128)(2,1)} %cot_hbm.1, s32[1,2048]{1,0:T(1,128)} %bitcast.3, bf16[3,3,32,32]{3,2,1,0:T(8,128)(2,1)} %wconv_hbm.1, bf16[32,32]{1,0:T(8,128)(2,1)} %wpoint_hbm.1, f32[1,32]{1,0:T(1,128)} %bitcast.4), custom_call_target="tpu_custom_call" | custom-call | flops 5400000000 | bytes 3145728 | tf_op jit(solution)/shard_map/pallas_call | solution.py:689
  68.0 2.1 %shard_map.94 = (bf16[32,64,256]{2,1,0:T(8,128)(2,1)}, f32[3,3,32,32]{3,2,1,0:T(8,128)}, f32[32,32]{1,0:T(8,128)}, f32[1,32]{1,0:T(1,128)}) custom-call(bf16[32,64,256]{2,1,0:T(8,128)(2,1)} %get-tuple-element.10.fg_hbm, f32[12,8,128]{2,1,0:T(8,128)} %get-tuple-element.11.sums_hbm), custom_call_target="tpu_custom_call" | custom-call | tf_op jit(solution)/shard_map/pallas_call | solution.py:752

commit v2 on v1

--- a/solution.py
+++ b/solution.py
@@ -405,7 +405,8 @@
     psum[...] = jnp.zeros_like(psum)
     bsum[...] = jnp.zeros_like(bsum)
 
-    each(1, pass_on)
+    for part in range(1, len(SLICES)):
+        each(part, pass_on)
     for copy in halo_copies(0):
         copy.wait_recv()
     act_fill()
@@ -491,7 +492,7 @@
 
     lax.fori_loop(0, 4, chunk, 0)
 
-    def exchange(stage, me, member, source, dst):
+    def exchange(stage, me, member, order, source, dst):
         def copy(to):
             return pltpu.make_async_remote_copy(
                 src_ref=source(to),
@@ -502,9 +503,9 @@
                 device_id_type=MESH,
             )
 
-        def start(d, _):
-            copy(lax.rem(me + d, GROUP)).start()
-            return 0
+        def start():
+            for to in order:
+                copy(to).start()
 
         def wait(sem):
             others = dst.at[0 : GROUP - 1]
@@ -512,14 +513,24 @@
 
         return (
             copy,
-            lambda: lax.fori_loop(1, GROUP, start, 0),
+            start,
             lambda: wait(red_rsem),
             lambda: wait(red_ssem),
         )
 
-    first_copy, _, arrive1, leave1 = exchange(0, group_b, member_b, lambda m: payload.at[m], part1)
-    _, start2, arrive2, leave2 = exchange(1, group_a, member_a, lambda m: sum1, part2)
-    _, start3, arrive3, leave3 = exchange(2, group_b, member_b, lambda m: sum2, part3)
+    def hops(d, ring):
+        return min(d, ring - d)
+
+    def far_first(rings):
+        offsets = [(i, j) for i in range(rings[0]) for j in range(rings[1])]
+        return sorted(offsets, key=lambda o: -hops(o[0], rings[0]) - hops(o[1], rings[1]))[:-1]
+
+    z, core = lax.div(group_a, 2), lax.rem(group_a, 2)
+    order_a = [2 * lax.rem(z + i, 8) + lax.rem(core + j, 2) for i, j in far_first((8, 2))]
+    order_b = [4 * lax.rem(y + i, 4) + lax.rem(b + j, 4) for i, j in far_first((4, 4))]
+    first_copy, _, arrive1, leave1 = exchange(0, group_b, member_b, order_b, lambda m: payload.at[m], part1)
+    _, start2, arrive2, leave2 = exchange(1, group_a, member_a, order_a, lambda m: sum1, part2)
+    _, start3, arrive3, leave3 = exchange(2, group_b, member_b, order_b, lambda m: sum2, part3)
 
     def send_payload(m):
         @pl.when(group_b == m)

time: 70.2 us -> 69.8 us (level)
  no operation moved by 1% of the time
where the time goes in v2:
time: 69.8 us; the launch traced here: 69.7 us
  Pallas kernels  69 us (99%)
    pallas_call x1, Pallas kernels, shards(): pl.pallas_call(kernel, out_shape=(jax.ShapeDtypeStruct((32, 64, 256), BF1...  67 us
    pallas_call x1, Pallas kernels, shards(): pl.pallas_call(finish, out_shape=(jax.ShapeDtypeStruct((32, 64, 256), BF1...  2.09 us

profile of v2, /device:TPU:1, one launch (start us, length us, event | category | flops | bytes accessed | tf_op | source)
XLA Modules:
  0.0 69.7 jit_solution(13407890065170680348)
XLA Ops:
  0.6 67.0 %shard_map.93 = (bf16[32,64,256]{2,1,0:T(8,128)(2,1)}, f32[12,8,128]{2,1,0:T(8,128)}) custom-call(bf16[32,64,256]{2,1,0:T(8,128)(2,1)} %feat_hbm.1, bf16[32,64,256]{2,1,0:T(8,128)(2,1)} %cot_hbm.1, s32[1,2048]{1,0:T(1,128)} %bitcast.3, bf16[3,3,32,32]{3,2,1,0:T(8,128)(2,1)} %wconv_hbm.1, bf16[32,32]{1,0:T(8,128)(2,1)} %wpoint_hbm.1, f32[1,32]{1,0:T(1,128)} %bitcast.4), custom_call_target="tpu_custom_call" | custom-call | flops 5400000000 | bytes 3145728 | tf_op jit(solution)/shard_map/pallas_call | solution.py:700
  67.6 2.1 %shard_map.94 = (bf16[32,64,256]{2,1,0:T(8,128)(2,1)}, f32[3,3,32,32]{3,2,1,0:T(8,128)}, f32[32,32]{1,0:T(8,128)}, f32[1,32]{1,0:T(1,128)}) custom-call(bf16[32,64,256]{2,1,0:T(8,128)(2,1)} %get-tuple-element.10.fg_hbm, f32[12,8,128]{2,1,0:T(8,128)} %get-tuple-element.11.sums_hbm), custom_call_target="tpu_custom_call" | custom-call | tf_op jit(solution)/shard_map/pallas_call | solution.py:763

commit v3 on v2

--- a/solution.py
+++ b/solution.py
@@ -13,7 +13,7 @@
 TILES = 8
 GROUP = 16
 FIRST, SECOND = 2, 5
-SLICES = ((0, 3), (3, 1))
+SLICES = ((0, 2), (2, 1), (3, 1))
 NT = (((1,), (1,)), ((), ()))
 TN = (((0,), (0,)), ((), ()))
 

time: 69.8 us -> 69.6 us (level)
  no operation moved by 1% of the time
where the time goes in v3:
time: 69.6 us; the launch traced here: 69.5 us
  Pallas kernels  68.8 us (99%)
    pallas_call x1, Pallas kernels, shards(): pl.pallas_call(kernel, out_shape=(jax.ShapeDtypeStruct((32, 64, 256), BF1...  66.7 us
    pallas_call x1, Pallas kernels, shards(): pl.pallas_call(finish, out_shape=(jax.ShapeDtypeStruct((32, 64, 256), BF1...  2.09 us

profile of v3, /device:TPU:1, one launch (start us, length us, event | category | flops | bytes accessed | tf_op | source)
XLA Modules:
  0.0 69.5 jit_solution(13424007831497369750)
XLA Ops:
  0.6 66.7 %shard_map.93 = (bf16[32,64,256]{2,1,0:T(8,128)(2,1)}, f32[12,8,128]{2,1,0:T(8,128)}) custom-call(bf16[32,64,256]{2,1,0:T(8,128)(2,1)} %feat_hbm.1, bf16[32,64,256]{2,1,0:T(8,128)(2,1)} %cot_hbm.1, s32[1,2048]{1,0:T(1,128)} %bitcast.3, bf16[3,3,32,32]{3,2,1,0:T(8,128)(2,1)} %wconv_hbm.1, bf16[32,32]{1,0:T(8,128)(2,1)} %wpoint_hbm.1, f32[1,32]{1,0:T(1,128)} %bitcast.4), custom_call_target="tpu_custom_call" | custom-call | flops 5400000000 | bytes 3145728 | tf_op jit(solution)/shard_map/pallas_call | solution.py:700
  67.4 2.1 %shard_map.94 = (bf16[32,64,256]{2,1,0:T(8,128)(2,1)}, f32[3,3,32,32]{3,2,1,0:T(8,128)}, f32[32,32]{1,0:T(8,128)}, f32[1,32]{1,0:T(1,128)}) custom-call(bf16[32,64,256]{2,1,0:T(8,128)(2,1)} %get-tuple-element.10.fg_hbm, f32[12,8,128]{2,1,0:T(8,128)} %get-tuple-element.11.sums_hbm), custom_call_target="tpu_custom_call" | custom-call | tf_op jit(solution)/shard_map/pallas_call | solution.py:763
